TPU v7x, 32 devices: a whole 2x2x4 slice. The times are simulated.
32 devices in a mesh: group: 2 (over y), outer: 4 (over z), seq: 4 (over x, core).
Axes of the slice: x: 2, y: 2, z: 4, core: 2. Of those that a mesh axis runs over, the one named last changes fastest.
Arguments:
- activations: bfloat16 [8, 512, 2048], P(('group', 'outer'), 'seq'), parts along dimension 0
- cotangent: bfloat16 [8, 512, 2048], P(('group', 'outer'), None, 'seq'), parts along dimension 0
- weights: bfloat16 [8, 2048, 2048], P(('group', 'outer'), None, 'seq'), parts along dimension 0
- earlier_delta: bfloat16 [8, 2048, 2048], P(('group', 'outer'), None, 'seq'), parts along dimension 0, may hold values from -6 to 6
- momentum: bfloat16 [8, 2048, 2048], P(('group', 'outer'), None, 'seq'), parts along dimension 0, may hold values from -3 to 3
- module_path: int32 [8], P('group'), parts along dimension 0, may hold values from 0 to 3
Outputs:
- new_weights: bfloat16 [8, 2048, 2048], P(('group', 'outer'), None, 'seq'), parts along dimension 0
- outer_delta: bfloat16 [8, 2048, 2048], P(('group', 'outer'), None, 'seq'), parts along dimension 0
- new_momentum: bfloat16 [8, 2048, 2048], P(('group', 'outer'), None, 'seq'), parts along dimension 0
There are 2 independent parts, one for each index of `group`. A program takes and returns all parts, laid end to end along the dimension named above; each array names one. Nothing has to cross between parts.
All inputs are finite; a program needn't handle non-finite values.
Results may differ from a plain program's by a relative error of at most 0.0036.
Values may be sent and summed in bfloat16 or wider, within the bound.
A program may use at most 128 MiB of HBM per device.

v0:
```python
import jax
import jax.numpy as jnp
from jax import lax
from jax.sharding import PartitionSpec as P

STEPS = 3


epsilon = 1e-06
inner_rate = 0.05
outer_rate = 0.7
beta_outer = 0.9


def body(activations, cotangent, weights, earlier_delta, momentum, module_path):
    gathered = lax.all_gather(activations[0], "seq", axis=0, tiled=True)
    width = gathered.shape[1]
    factor = 1.0 / jnp.sqrt(jnp.float32(width))
    own_pod = lax.axis_index("outer")
    matches = module_path[:, None] == module_path[None, :]
    shared_bf = jnp.where(matches, 1.0, 0.0).astype(jnp.bfloat16)
    group_size = jnp.sum(jnp.where(matches, 1.0, 0.0).astype(jnp.float32), axis=1)
    own_size = lax.dynamic_index_in_dim(group_size, own_pod, 0, keepdims=False)
    columns = weights.shape[2]
    npods = lax.axis_size("outer")
    blocks = earlier_delta[0].reshape(npods, width // npods, columns)
    sums = jnp.einsum(
        "pq,qrc->prc",
        shared_bf,
        lax.all_to_all(blocks, "outer", split_axis=0, concat_axis=0, tiled=True),
        preferred_element_type=jnp.float32,
    )
    returned = lax.all_to_all(sums, "outer", split_axis=0, concat_axis=0, tiled=True)
    summed = returned.reshape(width, columns)
    outer_grad = summed / own_size
    moment = beta_outer * momentum[0].astype(jnp.float32) + outer_grad
    direction = outer_grad + beta_outer * moment
    sensed = cotangent[0]
    current = weights[0].astype(jnp.float32)
    for inner_step in range(STEPS):
        weight_bf = current.astype(jnp.bfloat16)
        projected = jnp.dot(gathered, weight_bf, preferred_element_type=jnp.float32) * factor
        squares = lax.psum(jnp.sum(projected * projected, axis=1), "seq")
        row_rms = jnp.sqrt(squares / width + epsilon)[:, None]
        normed = projected / row_rms
        sigmoid_y = jax.nn.sigmoid(normed)
        grad_out = sensed.astype(jnp.float32) * sigmoid_y * (1.0 + normed * (1.0 - sigmoid_y))
        products = lax.psum(jnp.sum(grad_out * normed, axis=1), "seq")
        grad_in = ((grad_out - normed * (products / width)[:, None]) / row_rms).astype(jnp.bfloat16)
        gradient = (
            lax.dot_general(
                gathered, grad_in, (((0,), (0,)), ((), ())), preferred_element_type=jnp.float32
            )
            * factor
        )
        current = current - inner_rate * gradient
    outer_delta = ((weights[0].astype(jnp.float32) - current) / (inner_rate * STEPS)).astype(
        jnp.bfloat16
    )
    new_weights = (current - outer_rate * inner_rate * STEPS * direction).astype(jnp.bfloat16)
    new_momentum = moment.astype(jnp.bfloat16)
    return (new_weights[None], outer_delta[None], new_momentum[None])


def solution(mesh):
    in_specs = (
        P(("group", "outer"), "seq", None),
        P(("group", "outer"), None, "seq"),
        P(("group", "outer"), None, "seq"),
        P(("group", "outer"), None, "seq"),
        P(("group", "outer"), None, "seq"),
        P("group"),
    )
    out_specs = (
        P(("group", "outer"), None, "seq"),
        P(("group", "outer"), None, "seq"),
        P(("group", "outer"), None, "seq"),
    )
    return jax.shard_map(body, mesh=mesh, in_specs=in_specs, out_specs=out_specs, check_vma=False)
```

profile of v0, /device:TPU:0, one launch (start us, length us, event | category | flops | bytes accessed | tf_op | source)
XLA Modules:
  0.0 213.1 jit_solution(14805752611587819355)
XLA Ops:
  7.2 6.3 %all-to-all-start = ((bf16[4,512,512]{2,1,0:T(8,128)(2,1)}), bf16[4,512,512]{2,1,0:T(8,128)(2,1)S(1)}, u32[]{:S(2)}, u32[]{:S(2)}) async-start(bf16[4,512,512]{2,1,0:T(8,128)(2,1)} %bitcast.153), calls=%async_computation | async-start | bytes 4194304 | tf_op jit(solution)/shard_map/all_to_all | solution.py:30
  13.5 0.7 all-gather.3.cloned.1.call-update
  14.2 47.5 %all-to-all-done = bf16[4,512,512]{2,1,0:T(8,128)(2,1)S(1)} async-done(((bf16[4,512,512]{2,1,0:T(8,128)(2,1)}), bf16[4,512,512]{2,1,0:T(8,128)(2,1)S(1)}, u32[]{:S(2)}, u32[]{:S(2)}) %all-to-all-start) | async-done | bytes 2097184 | tf_op jit(solution)/shard_map/all_to_all | solution.py:30
  61.7 1.8 fusion.19
  63.5 3.2 %copy.32 = f32[4,512,512]{2,1,0:T(8,128)} copy(f32[4,512,512]{2,0,1:T(4,128)S(1)} %fusion.19) | data formatting | bytes 8388608 | tf_op jit(solution)/shard_map/pq,qrc->prc/dot_general | solution.py:27
  66.7 5.1 %all-to-all-start.1 = ((f32[4,512,512]{2,1,0:T(8,128)}), f32[4,512,512]{2,1,0:T(8,128)}, u32[]{:S(2)}, u32[]{:S(2)}) async-start(f32[4,512,512]{2,1,0:T(8,128)} %copy.32), calls=%async_computation.1 | async-start | bytes 8388608 | tf_op jit(solution)/shard_map/all_to_all | solution.py:33
  72.0 2.9 %copy.34 = bf16[1,2048,512]{1,2,0:T(8,128)(2,1)S(1)} copy(bf16[1,2048,512]{2,1,0:T(8,128)(2,1)} %param.10) | data formatting | bytes 4194304 | tf_op args[4]
  74.9 3.9 %copy.28 = bf16[1,2048,512]{1,2,0:T(8,128)(2,1)} copy(bf16[1,2048,512]{2,1,0:T(8,128)(2,1)} %param.8) | data formatting | bytes 4194304 | tf_op args[2]
  79.0 0.6 dynamic_slice.4
  79.6 4.5 %multiply_reduce_fusion.3 = (f32[512]{0:T(512)S(1)}, f32[512,512]{0,1:T(8,128)}) fusion(bf16[1,2048,512]{2,1,0:T(8,128)(2,1)} %param.8, bf16[1,512,2048]{2,1,0:T(8,128)(2,1)} %all-gather.3.cloned.1.call-done), kind=kOutput, calls=%fused_computation.68 | convolution fusion | flops 1074527744 | bytes 5244928 | tf_op jit(solution)/shard_map/dot_general | solution.py:42
  84.1 6.2 %psum.42 = f32[512]{0:T(512)S(1)} all-reduce(f32[512]{0:T(512)S(1)} %get-tuple-element.14), channel_id=1, replica_groups=mesh['group'=2,'outer'=4,'seq'=4] {'seq'}, use_global_device_ids=true, to_apply=%region_1.2 | all-reduce | flops 512 | bytes 4096 | tf_op jit(solution)/shard_map/psum | solution.py:43
  90.3 1.7 multiply_reduce_fusion.2
  92.0 6.5 %psum.43 = f32[512]{0:T(512)S(1)} all-reduce(f32[512]{0:T(512)S(1)} %multiply_reduce_fusion.2), channel_id=1, replica_groups=mesh['group'=2,'outer'=4,'seq'=4] {'seq'}, use_global_device_ids=true, to_apply=%region_3.4 | all-reduce | flops 512 | bytes 4096 | tf_op jit(solution)/shard_map/psum | solution.py:48
  98.5 4.3 %convert_subtract_fusion.1 = f32[2048,512]{0,1:T(8,128)S(1)} fusion(bf16[1,512,2048]{2,1,0:T(8,128)(2,1)} %all-gather.3.cloned.1.call-done, bf16[1,2048,512]{1,2,0:T(8,128)(2,1)} %copy.28, bf16[1,512,512]{1,2,0:T(8,128)(2,1)S(1)} %copy.29, f32[512]{0:T(512)S(1)} %broadcast_multiply_fusion.2, f32[512]{0:T(512)S(1)} %add_sqrt_fusion.2, ...), kind=kOutput, calls=%fused_computation.1 | convolution fusion | flops 1080557568 | bytes 9965568 | tf_op jit(solution)/shard_map/dot_general | solution.py:51
  102.8 2.3 %multiply_reduce_fusion.1 = (f32[512]{0:T(512)S(1)}, f32[512,512]{1,0:T(8,128)}) fusion(bf16[1,512,2048]{2,1,0:T(8,128)(2,1)S(1)} %copy-done.2, f32[2048,512]{0,1:T(8,128)S(1)} %convert_subtract_fusion.1), kind=kOutput, calls=%fused_computation.65 | convolution fusion | flops 1075576320 | bytes 7342080 | tf_op jit(solution)/shard_map/dot_general | solution.py:42
  105.1 6.0 %psum.44 = f32[512]{0:T(512)S(1)} all-reduce(f32[512]{0:T(512)S(1)} %get-tuple-element.16), channel_id=1, replica_groups=mesh['group'=2,'outer'=4,'seq'=4] {'seq'}, use_global_device_ids=true, to_apply=%region_5.6 | all-reduce | flops 512 | bytes 4096 | tf_op jit(solution)/shard_map/psum | solution.py:43
  111.2 1.7 fusion.53
  112.9 6.2 %psum.45 = f32[512]{0:T(512)S(1)} all-reduce(f32[512]{0:T(512)S(1)} %fusion.53), channel_id=1, replica_groups=mesh['group'=2,'outer'=4,'seq'=4] {'seq'}, use_global_device_ids=true, to_apply=%region_7.8 | all-reduce | flops 512 | bytes 4096 | tf_op jit(solution)/shard_map/psum | solution.py:48
  119.1 4.9 %bitcast_subtract_fusion.1 = f32[2048,512]{0,1:T(8,128)S(1)} fusion(f32[2048,512]{0,1:T(8,128)} %copy-done.5, bf16[1,512,2048]{2,1,0:T(8,128)(2,1)} %all-gather.3.cloned.1.call-done, bf16[1,512,512]{1,2,0:T(8,128)(2,1)S(1)} %copy.29, f32[512]{0:T(512)S(1)} %add_sqrt_fusion.1, f32[512]{0:T(512)S(1)} %broadcast_multiply_fusion.1, ...), kind=kOutput, calls=%fused_computation.11 | convolution fusion | flops 1079508992 | bytes 12062720 | tf_op jit(solution)/shard_map/dot_general | solution.py:51
  124.1 2.3 %multiply_reduce_fusion = (f32[512]{0:T(512)S(1)}, f32[512,512]{1,0:T(8,128)}) fusion(bf16[1,512,2048]{2,1,0:T(8,128)(2,1)S(1)} %copy-done.3, f32[2048,512]{0,1:T(8,128)S(1)} %bitcast_subtract_fusion.1), kind=kOutput, calls=%fused_computation.64 | convolution fusion | flops 1075576320 | bytes 7342080 | tf_op jit(solution)/shard_map/dot_general | solution.py:42
  126.4 5.6 %psum.46 = f32[512]{0:T(512)S(1)} all-reduce(f32[512]{0:T(512)S(1)} %get-tuple-element.18), channel_id=1, replica_groups=mesh['group'=2,'outer'=4,'seq'=4] {'seq'}, use_global_device_ids=true, to_apply=%region_9.10 | all-reduce | flops 512 | bytes 4096 | tf_op jit(solution)/shard_map/psum | solution.py:43
  132.1 1.7 fusion.45
  133.8 6.4 %psum.47 = f32[512]{0:T(512)S(1)} all-reduce(f32[512]{0:T(512)S(1)} %fusion.45), channel_id=1, replica_groups=mesh['group'=2,'outer'=4,'seq'=4] {'seq'}, use_global_device_ids=true, to_apply=%region_11.12 | all-reduce | flops 512 | bytes 4096 | tf_op jit(solution)/shard_map/psum | solution.py:48
  140.2 24.3 %all-to-all-done.1 = f32[4,512,512]{2,1,0:T(8,128)} async-done(((f32[4,512,512]{2,1,0:T(8,128)}), f32[4,512,512]{2,1,0:T(8,128)}, u32[]{:S(2)}, u32[]{:S(2)}) %all-to-all-start.1) | async-done | bytes 4194336 | tf_op jit(solution)/shard_map/all_to_all | solution.py:33
  164.5 5.3 %broadcast_divide_fusion = f32[4,512,512]{2,1,0:T(8,128)} fusion(f32[4,512,512]{2,1,0:T(8,128)} %all-to-all-done.1, f32[]{:T(128)} %bitcast.11), kind=kLoop, calls=%fused_computation.28 | loop fusion | flops 1048576 | bytes 8388612 | tf_op jit(solution)/shard_map/div | solution.py:35
  169.7 5.4 %copy.39 = f32[2048,512]{0,1:T(8,128)} copy(f32[2048,512]{1,0:T(8,128)} %bitcast.151) | data formatting | bytes 8388608 | tf_op jit(solution)/shard_map/div | solution.py:35
  175.1 9.7 %fusion.8 = (bf16[1,2048,512]{1,2,0:T(8,128)(2,1)}, bf16[1,2048,512]{1,2,0:T(8,128)(2,1)}) fusion(bf16[1,2048,512]{1,2,0:T(8,128)(2,1)} %copy.28, f32[2048,512]{0,1:T(8,128)} %copy.39, bf16[1,2048,512]{1,2,0:T(8,128)(2,1)S(1)} %copy.34, f32[2048,512]{0,1:T(8,128)} %copy-done.4, bf16[1,512,2048]{2,1,0:T(8,128)(2,1)} %all-gather.3.cloned.1.call-done, ...), kind=kOutput, calls=%fused_computation.15 | convolution fusion | flops 1092091904 | bytes 20451328 | tf_op jit(solution)/shard_map/dot_general | solution.py:51
  184.8 3.9 %copy.37 = bf16[1,2048,512]{2,1,0:T(8,128)(2,1)} copy(bf16[1,2048,512]{1,2,0:T(8,128)(2,1)} %get-tuple-element.12) | data formatting | bytes 4194304
  188.8 3.9 %copy.36 = bf16[1,2048,512]{2,1,0:T(8,128)(2,1)} copy(bf16[1,2048,512]{1,2,0:T(8,128)(2,1)} %get-tuple-element.13) | data formatting | bytes 4194304
  192.7 5.4 %copy.40 = f32[1,2048,512]{1,2,0:T(8,128)} copy(f32[1,2048,512]{2,1,0:T(8,128)} %bitcast.152) | data formatting | bytes 8388608 | tf_op jit(solution)/shard_map/div | solution.py:35
  198.1 4.3 %add_convert_fusion = bf16[1,2048,512]{1,2,0:T(8,128)(2,1)} fusion(f32[1,2048,512]{1,2,0:T(8,128)} %copy.40, bf16[1,2048,512]{1,2,0:T(8,128)(2,1)S(1)} %copy.34), kind=kLoop, calls=%fused_computation.12 | loop fusion | flops 4194304 | bytes 8388608 | tf_op jit(solution)/shard_map/convert_element_type | solution.py:61
  202.4 3.9 %copy.38 = bf16[1,2048,512]{2,1,0:T(8,128)(2,1)} copy(bf16[1,2048,512]{1,2,0:T(8,128)(2,1)} %add_convert_fusion) | data formatting | bytes 4194304
  (22 shorter events, 0.5 us)
Async XLA Ops:
  7.2 54.5 %copy-start.1 = (s32[4]{0:T(128)S(1)}, s32[4]{0:T(128)}, u32[]{:S(2)}) copy-start(s32[4]{0:T(128)} %param.11) | copy-start | bytes 52
  7.2 54.5 %all-to-all-start = ((bf16[4,512,512]{2,1,0:T(8,128)(2,1)}), bf16[4,512,512]{2,1,0:T(8,128)(2,1)S(1)}, u32[]{:S(2)}, u32[]{:S(2)}) async-start(bf16[4,512,512]{2,1,0:T(8,128)(2,1)} %bitcast.153), calls=%async_computation | async-start | bytes 4194304 | tf_op jit(solution)/shard_map/all_to_all | solution.py:30
  13.5 66.1 %all-gather.3.cloned.1.call-start = ((), (), s32[]{:S(2)}) async-start(), calls=%async_computation.2 | async-start | bytes 2621440 | tf_op jit(solution)/shard_map/all_gather | solution.py:16
  66.7 5.1 %copy-start = (bf16[1,512,512]{2,1,0:T(8,128)(2,1)S(1)}, bf16[1,512,512]{2,1,0:T(8,128)(2,1)}, u32[]{:S(2)}) copy-start(bf16[1,512,512]{2,1,0:T(8,128)(2,1)} %param.7) | copy-start | bytes 1572868
  66.7 97.8 %all-to-all-start.1 = ((f32[4,512,512]{2,1,0:T(8,128)}), f32[4,512,512]{2,1,0:T(8,128)}, u32[]{:S(2)}, u32[]{:S(2)}) async-start(f32[4,512,512]{2,1,0:T(8,128)} %copy.32), calls=%async_computation.1 | async-start | bytes 8388608 | tf_op jit(solution)/shard_map/all_to_all | solution.py:33
  98.5 4.3 %copy-start.2 = (bf16[1,512,2048]{2,1,0:T(8,128)(2,1)S(1)}, bf16[1,512,2048]{2,1,0:T(8,128)(2,1)}, u32[]{:S(2)}) copy-start(bf16[1,512,2048]{2,1,0:T(8,128)(2,1)} %all-gather.3.cloned.1.call-done) | copy-start | bytes 6291460
  102.8 2.4 %copy-start.5 = (f32[2048,512]{0,1:T(8,128)}, f32[2048,512]{0,1:T(8,128)S(1)}, u32[]{:S(2)}) copy-start(f32[2048,512]{0,1:T(8,128)S(1)} %convert_subtract_fusion.1) | copy-start | bytes 12582916
  119.1 4.9 %copy-start.3 = (bf16[1,512,2048]{2,1,0:T(8,128)(2,1)S(1)}, bf16[1,512,2048]{2,1,0:T(8,128)(2,1)}, u32[]{:S(2)}) copy-start(bf16[1,512,2048]{2,1,0:T(8,128)(2,1)} %all-gather.3.cloned.1.call-done) | copy-start | bytes 6291460
  124.0 2.4 %copy-start.4 = (f32[2048,512]{0,1:T(8,128)}, f32[2048,512]{0,1:T(8,128)S(1)}, u32[]{:S(2)}) copy-start(f32[2048,512]{0,1:T(8,128)S(1)} %bitcast_subtract_fusion.1) | copy-start | bytes 12582916
Sparse Core Ops, SparseCore 0:
  15.9 24.0 all-gather.2
where the time goes:
time: 214 us; the launch traced here: 213 us
  waiting for transfers between devices  72.4 us (34%)
  blocking collectives  37 us (17%)
  local copies, waits for them, and re-layouts  33.5 us (16%)
  matrix products  29.8 us (14%)
  other arithmetic  14.9 us (7%)
  between operations  14.1 us (7%)
  starting transfers between devices  11.4 us (5%)
    all_to_all x1, waiting for transfers between devices, body(): lax.all_to_all(blocks, 'outer', split_axis=0, concat_axis=0, tiled=True)  47.5 us
    all_to_all x1, waiting for transfers between devices, body(): lax.all_to_all(sums, 'outer', split_axis=0, concat_axis=0, tiled=True)  24.3 us
    psum x3, blocking collectives, body(): products = lax.psum(jnp.sum(grad_out * normed, axis=1), 'seq')  19.2 us
    dot_general x3, matrix products, body(): lax.dot_general(gathered, grad_in, (((0,), (0,)), ((), ())), preferred_el...  18.9 us
    unnamed x18, local copies, waits for them, and re-layouts  18.8 us
    psum x3, blocking collectives, body(): squares = lax.psum(jnp.sum(projected * projected, axis=1), 'seq')  17.9 us
    div x2, local copies, waits for them, and re-layouts, body(): outer_grad = summed / own_size  10.8 us
    dot_general x3, matrix products, body(): jnp.dot(gathered, weight_bf, preferred_element_type=jnp.float32) * factor  9.17 us
  transfers between devices with their start and end apart: 3, of which 2 were waited for; matrix products, arithmetic and copies ran while one was open for 17% of the time, Pallas kernels for 0%

commit v1 on v0

--- a/solution.py
+++ b/solution.py
@@ -1,6 +1,10 @@
+import functools
+
 import jax
 import jax.numpy as jnp
 from jax import lax
+from jax.experimental import pallas as pl
+from jax.experimental.pallas import tpu as pltpu
 from jax.sharding import PartitionSpec as P
 
 STEPS = 3
@@ -10,6 +14,361 @@
 inner_rate = 0.05
 outer_rate = 0.7
 beta_outer = 0.9
+
+MESH = pl.DeviceIdType.MESH
+PIECES = 16
+F32 = jnp.float32
+BF16 = jnp.bfloat16
+
+
+def kernel(slots, coef, a_hbm, c_hbm, w_hbm, d_hbm, m_hbm, ow_hbm, od_hbm, om_hbm,
+           a, c, w, d, m, e, y1, y2, z, proj, normed, sens, gram, grads, cur, ow, od, om,
+           sent, sums, load, agx_s, agx_r, agc_s, agc_r, agf_s, agf_r, ex_s, ex_r,
+           e_s, e_r, y1_s, y1_r, y2_s, y2_r, z_s, z_r, out_s):
+    tokens, width = a.shape
+    columns = w.shape[1]
+    shard = tokens // 4
+    half = tokens // 2
+    rows = width // PIECES
+    factor = 1.0 / width ** 0.5
+
+    o = lax.axis_index("outer")
+    s = lax.axis_index("seq")
+    core = s % 2
+    chip = s // 2
+    peers = (chip * 2 + 1 - core, (1 - chip) * 2 + core, (1 - chip) * 2 + 1 - core)
+    near = o + 1 - 2 * (o % 2)
+    mid = 3 - o
+    inner = jnp.logical_or(o == 1, o == 2)
+    end = jnp.logical_or(o == 0, o == 3)
+
+    def remote(src, dst, send, recv, **where):
+        return pltpu.make_async_remote_copy(
+            src_ref=src, dst_ref=dst, send_sem=send, recv_sem=recv, device_id=where, device_id_type=MESH)
+
+    barrier = pltpu.get_barrier_semaphore()
+    for peer in peers:
+        pl.semaphore_signal(barrier, inc=1, device_id={"seq": peer}, device_id_type=MESH)
+    pl.semaphore_signal(barrier, inc=1, device_id={"outer": near}, device_id_type=MESH)
+
+    @pl.when(inner)
+    def _():
+        pl.semaphore_signal(barrier, inc=1, device_id={"outer": mid}, device_id_type=MESH)
+
+    local = [pltpu.make_async_copy(x, y, load.at[k]) for k, (x, y) in enumerate(
+        ((a_hbm, a.at[pl.ds(pl.multiple_of(s * shard, shard), shard)]), (w_hbm, w), (c_hbm, c), (d_hbm, d), (m_hbm, m)))]
+    for copy in local:
+        copy.start()
+
+    @pl.when(inner)
+    def _():
+        pl.semaphore_wait(barrier, 5)
+
+    @pl.when(end)
+    def _():
+        pl.semaphore_wait(barrier, 4)
+
+    parts = 4
+    piece = shard // parts
+
+    def rows_of(owner, k):
+        return pl.ds(pl.multiple_of(owner * shard + k * piece, piece), piece)
+
+    def to_chip(k):
+        return remote(a_hbm.at[pl.ds(k * piece, piece)], a.at[rows_of(s, k)], agx_s.at[k], agx_r.at[k], seq=peers[1])
+
+    def forward(k):
+        return remote(a.at[rows_of(peers[1], k)], a.at[rows_of(peers[1], k)], agf_s.at[k], agf_r.at[k], seq=peers[0])
+
+    own_rows = pl.ds(pl.multiple_of(s * shard, shard), shard)
+    to_core = remote(a_hbm, a.at[own_rows], agc_s, agc_r, seq=peers[0])
+    for k in range(parts):
+        to_chip(k).start()
+    to_core.start()
+
+    def span(k):
+        return pl.ds(pl.multiple_of(k * rows, rows), rows)
+
+    def send_e(k):
+        return remote(d_hbm.at[span(k)], e.at[span(k)], e_s.at[k], e_r.at[k], outer=near)
+
+    def send_y1(k):
+        return remote(d_hbm.at[span(k)] if slots == 2 else y2.at[span(k)], y1.at[span(k)],
+                      y1_s.at[k], y1_r.at[k], outer=mid)
+
+    def send_y2(k):
+        return remote(e.at[span(k)], y2.at[span(k)], y2_s.at[k], y2_r.at[k], outer=mid)
+
+    def send_z(k):
+        return remote(z.at[span(k)], e.at[span(k)], z_s.at[k], z_r.at[k], outer=near)
+
+    def loop(lo, hi, body):
+        def step(k, carry):
+            body(k)
+            return carry
+        lax.fori_loop(lo, hi, step, 0)
+
+    @pl.when(end)
+    def _():
+        loop(0, PIECES, lambda k: send_e(k).start())
+
+    if slots == 2:
+        @pl.when(inner)
+        def _():
+            loop(0, PIECES, lambda k: send_y1(k).start())
+
+    def combine(k):
+        send_e(k).wait_recv()
+        y2[span(k)] = (coef[7] * e[span(k)].astype(F32) + coef[8] * d[span(k)].astype(F32)).astype(BF16)
+        send_y1(k).start()
+
+    def pass_on(k):
+        send_y1(k).wait_recv()
+        total = coef[4] * d[span(k)].astype(F32) + coef[5] * y1[span(k)].astype(F32)
+        if slots == 2:
+            send_y2(k).wait_recv()
+            total = total + coef[6] * y2[span(k)].astype(F32)
+        z[span(k)] = total.astype(BF16)
+        send_z(k).start()
+
+    lag = 2
+
+    def tick(lo, hi):
+        if slots == 1:
+            @pl.when(inner)
+            def _():
+                loop(lo, min(hi, PIECES), combine)
+                loop(max(lo - lag, 0), hi - lag, pass_on)
+
+    for copy in local:
+        copy.wait()
+
+    def project(block):
+        r = pl.ds(pl.multiple_of(block * half, half), half)
+        tile = min(256, columns)
+
+        def one(k):
+            cols = pl.ds(pl.multiple_of(k * tile, tile), tile)
+            proj[r, cols] = jnp.dot(a[r, :], w[:, cols], preferred_element_type=F32) * factor
+        loop(0, columns // tile, one)
+
+    to_core.wait_recv()
+    project(chip)
+    tick(0, 1)
+    for k in range(parts):
+        to_chip(k).wait_recv()
+        forward(k).start()
+    tick(1, 3)
+    for k in range(parts):
+        forward(k).wait_recv()
+    project(1 - chip)
+
+    group = 128
+    groups = tokens // group
+    eye = lax.broadcasted_iota(jnp.int32, (group, group), 0) == lax.broadcasted_iota(jnp.int32, (group, group), 1)
+
+    def rows_at(g):
+        return pl.ds(pl.multiple_of(g * group, group), group)
+
+    def to_row(column):
+        return jnp.sum(jnp.where(eye, column, 0.0), axis=0, keepdims=True)
+
+    def to_column(row):
+        return jnp.sum(jnp.where(eye, row, 0.0), axis=1, keepdims=True)
+
+    def exchange(n, k):
+        return remote(sent.at[n], sums.at[n, k], ex_s.at[n, k], ex_r.at[n, k], seq=peers[k])
+
+    def post(n):
+        for k in range(3):
+            exchange(n, k).start()
+
+    def collect(n):
+        for k in range(3):
+            exchange(n, k).wait_recv()
+
+    def total(n, g):
+        one = pl.ds(g, 1)
+        return sent[n, one, :] + sums[n, 0, one, :] + sums[n, 1, one, :] + sums[n, 2, one, :]
+
+    def gram_tile(k):
+        r = pl.ds(pl.multiple_of(k * 256, 256), 256)
+        gram[:, r] = (lax.dot_general(a[...], a[r, :], (((1,), (1,)), ((), ())), preferred_element_type=F32)
+                      * (inner_rate / width)).astype(BF16)
+
+    points = ((3, 5), (5, 7), (7, 8), (8, 10), (10, 11), (11, 12))
+    for step in range(STEPS):
+        first, second = 2 * step, 2 * step + 1
+
+        def squares(g):
+            p = proj[rows_at(g), :]
+            sent[first, pl.ds(g, 1), :] = to_row(jnp.sum(p * p, axis=1, keepdims=True))
+        loop(0, groups, squares)
+        post(first)
+        if step == 0:
+            loop(0, tokens // 256, gram_tile)
+        tick(*points[first])
+        collect(first)
+
+        def inverse(g):
+            return to_column(lax.rsqrt(total(first, g) / width + epsilon))
+
+        def sensitivity(g):
+            n = proj[rows_at(g), :] * inverse(g)
+            sig = jax.nn.sigmoid(n)
+            out = c[rows_at(g), :].astype(F32) * sig * (1.0 + n * (1.0 - sig))
+            normed[rows_at(g), :] = n
+            sens[rows_at(g), :] = out
+            sent[second, pl.ds(g, 1), :] = to_row(jnp.sum(out * n, axis=1, keepdims=True))
+        loop(0, groups, sensitivity)
+        post(second)
+        tick(*points[second])
+        collect(second)
+
+        def gradient(g):
+            mixed = to_column(total(second, g) / width)
+            grads[step, rows_at(g), :] = (
+                (sens[rows_at(g), :] - normed[rows_at(g), :] * mixed) * inverse(g)).astype(BF16)
+        loop(0, groups, gradient)
+        if step < STEPS - 1:
+            def descend(k):
+                cols = pl.ds(pl.multiple_of(k * 256, 256), 256)
+                proj[:, cols] -= jnp.dot(gram[...], grads[step, :, cols], preferred_element_type=F32)
+            loop(0, columns // 256, descend)
+
+    def weight_rows(k):
+        r = pl.ds(pl.multiple_of(k * 256, 256), 256)
+        turned = a[:, r].T
+        acc = jnp.dot(turned, grads[0], preferred_element_type=F32)
+        for step in range(1, STEPS):
+            acc = acc + jnp.dot(turned, grads[step], preferred_element_type=F32)
+        od[r, :] = (acc * (factor / STEPS)).astype(BF16)
+        cur[r, :] = w[r, :].astype(F32) - acc * (inner_rate * factor)
+    loop(0, width // 256, weight_rows)
+    delta_out = pltpu.make_async_copy(od, od_hbm, out_s.at[2, 0])
+    delta_out.start()
+
+    def outs(k):
+        return (pltpu.make_async_copy(ow.at[span(k)], ow_hbm.at[span(k)], out_s.at[0, k]),
+                pltpu.make_async_copy(om.at[span(k)], om_hbm.at[span(k)], out_s.at[1, k]))
+
+    def finish(k, summed):
+        outer_grad = summed * coef[0]
+        moment = beta_outer * m[span(k)].astype(F32) + outer_grad
+        direction = outer_grad + beta_outer * moment
+        om[span(k)] = moment.astype(BF16)
+        ow[span(k)] = (cur[span(k)] - (outer_rate * inner_rate * STEPS) * direction).astype(BF16)
+        for copy in outs(k):
+            copy.start()
+
+    def finish_inner(k):
+        summed = d[span(k)].astype(F32) + coef[1] * e[span(k)].astype(F32) + coef[2] * y1[span(k)].astype(F32)
+        if slots == 2:
+            summed = summed + coef[3] * y2[span(k)].astype(F32)
+        finish(k, summed)
+
+    @pl.when(inner)
+    def _():
+        if slots == 2:
+            def relay(k):
+                send_e(k).wait_recv()
+                send_y2(k).start()
+            loop(0, PIECES, relay)
+
+            def both(k):
+                pass_on(k)
+                finish_inner(k)
+            loop(0, PIECES, both)
+        else:
+            done = points[-1][1]
+
+            def both(k):
+                @pl.when(k < PIECES)
+                def _():
+                    combine(k)
+                pass_on(k - lag)
+            loop(done, PIECES + lag, both)
+            loop(0, PIECES, finish_inner)
+
+        def settle(k):
+            send_y1(k).wait_send()
+            if slots == 2:
+                send_y2(k).wait_send()
+            send_z(k).wait_send()
+        loop(0, PIECES, settle)
+
+    @pl.when(end)
+    def _():
+        def last(k):
+            send_z(k).wait_recv()
+            finish(k, d[span(k)].astype(F32) + e[span(k)].astype(F32))
+        loop(0, PIECES, last)
+        loop(0, PIECES, lambda k: send_e(k).wait_send())
+
+    to_core.wait_send()
+    for k in range(parts):
+        to_chip(k).wait_send()
+        forward(k).wait_send()
+    for n in range(2 * STEPS):
+        for k in range(3):
+            exchange(n, k).wait_send()
+
+    def written(k):
+        for copy in outs(k):
+            copy.wait()
+    loop(0, PIECES, written)
+    delta_out.wait()
+
+
+def phase(slots, coef, activations, cotangent, weights, earlier_delta, momentum):
+    width, columns = weights.shape
+    tokens = cotangent.shape[0]
+    any_spec = pl.BlockSpec(memory_space=pl.ANY)
+    full = pltpu.VMEM((width, columns), BF16)
+    plane = pltpu.VMEM((tokens, columns), F32)
+    dma = pltpu.SemaphoreType.DMA
+    line = dma((PIECES,))
+    out = jax.ShapeDtypeStruct((width, columns), BF16)
+    return pl.pallas_call(
+        functools.partial(kernel, slots),
+        out_shape=(out, out, out),
+        in_specs=[pl.BlockSpec(memory_space=pltpu.SMEM)] + [any_spec] * 5,
+        out_specs=(any_spec,) * 3,
+        scratch_shapes=[
+            pltpu.VMEM((tokens, width), BF16), pltpu.VMEM((tokens, columns), BF16),
+            full, full, full, full, full, full, full,
+            plane, plane, plane, pltpu.VMEM((tokens, tokens), BF16),
+            pltpu.VMEM((STEPS, tokens, columns), BF16),
+            pltpu.VMEM((width, columns), F32), full, full, full,
+            pltpu.VMEM((2 * STEPS, 8, 128), F32), pltpu.VMEM((2 * STEPS, 3, 8, 128), F32),
+            dma((5,)), dma((4,)), dma((4,)), dma, dma, dma((4,)), dma((4,)),
+            dma((2 * STEPS, 3)), dma((2 * STEPS, 3)),
+            line, line, line, line, line, line, line, line, dma((3, PIECES)),
+        ],
+        compiler_params=pltpu.CompilerParams(
+            collective_id=slots, has_side_effects=True, vmem_limit_bytes=56 * 1024 * 1024),
+        cost_estimate=pl.CostEstimate(
+            flops=12 * tokens * width * columns, bytes_accessed=14 * width * columns, transcendentals=0),
+        name="phase%d" % slots,
+    )(coef, activations, cotangent, weights, earlier_delta, momentum)
+
+
+def line_body(activations, cotangent, weights, earlier_delta, momentum, module_path):
+    shared = (module_path[:, None] == module_path[None, :]).astype(F32)
+    own = lax.axis_index("outer")
+    near = own + 1 - 2 * (own % 2)
+    mid, far = 3 - own, 3 - near
+    side = jnp.arange(4) // 2
+    crosses = jnp.max(jnp.where(side[:, None] != side[None, :], shared, 0.0), axis=1)
+
+    def pair(i, j):
+        return shared[i, j]
+
+    wide = [1.0 / jnp.sum(shared[own]), pair(own, near), pair(own, mid), pair(own, far),
+            pair(near, own), pair(near, mid), pair(near, far), crosses[near], crosses[own]]
+    arrays = (activations[0], cotangent[0], weights[0], earlier_delta[0], momentum[0])
+    outs = phase(2, jnp.stack(wide), *arrays)
+    return tuple(x[None] for x in outs)
 
 
 def body(activations, cotangent, weights, earlier_delta, momentum, module_path):
@@ -76,4 +435,11 @@
         P(("group", "outer"), None, "seq"),
         P(("group", "outer"), None, "seq"),
     )
-    return jax.shard_map(body, mesh=mesh, in_specs=in_specs, out_specs=out_specs, check_vma=False)
+    def run(*args):
+        sizes = (mesh.shape["outer"], mesh.shape["seq"], args[0].shape[1], args[2].shape[1])
+        fits = sizes[:2] == (4, 4) and sizes[2] == 512 and sizes[3] % 512 == 0 and sizes[3] <= 2048
+        chosen = line_body if fits else body
+        return jax.shard_map(
+            chosen, mesh=mesh, in_specs=in_specs, out_specs=out_specs, check_vma=False)(*args)
+
+    return run

time: 214 us -> 122 us (0.57)
  Pallas kernels: 0 us -> 104 us
  waiting for transfers between devices: 72.4 us -> 0 us
  blocking collectives: 37 us -> 0 us
  matrix products: 29.8 us -> 0 us
  local copies, waits for them, and re-layouts: 33.5 us -> 13.8 us
  between operations: 14.1 us -> 1.37 us
  other arithmetic: 14.9 us -> 2.32 us
  starting transfers between devices: 11.4 us -> 0 us
    pallas_call x0 -> x1, Pallas kernels: none -> 104 us  [phase(): pl.pallas_call(functools.partial(kernel, slots), out_shape=(out, out, out...]
    all_to_all x2 -> x0, waiting for transfers between devices: 71.7 us -> none  [the longest x1 47.5 us: body(): lax.all_to_all(blocks, 'outer', split_axis=0, concat_axis=0, tiled=True)]
    psum x6 -> x0, blocking collectives: 37 us -> none  [the longest x3 19.2 us: body(): products = lax.psum(jnp.sum(grad_out * normed, axis=1), 'seq')]
    dot_general x7 -> x0, matrix products: 29.8 us -> none  [the longest x3 18.9 us: body(): lax.dot_general(gathered, grad_in, (((0,), (0,)), ((), ())), preferred_el...]
    unnamed x18 -> x7, local copies, waits for them, and re-layouts: 18.8 us -> 6.86 us
    all_to_all x2 -> x0, starting transfers between devices: 11.4 us -> none  [the longest x1 6.33 us: body(): lax.all_to_all(blocks, 'outer', split_axis=0, concat_axis=0, tiled=True)]
    div x2 -> x0, local copies, waits for them, and re-layouts: 10.8 us -> none  [body(): outer_grad = summed / own_size]
    another operation x0 -> x1, local copies, waits for them, and re-layouts: none -> 5.63 us  [line_body(): outs = phase(2, jnp.stack(wide), *arrays)]
  transfers between devices with their start and end apart: 3 -> 0, of which waited for: 2 -> 0; matrix products, arithmetic and copies ran while one was open for 17% -> 0% of each run, Pallas kernels for 0% -> 0%
where the time goes in v1:
time: 122 us
  Pallas kernels  104 us (85%)
  local copies, waits for them, and re-layouts  13.8 us (11%)
  other arithmetic  2.32 us (2%)
  between operations  1.37 us (1%)
    pallas_call x1, Pallas kernels, phase(): pl.pallas_call(functools.partial(kernel, slots), out_shape=(out, out, out...  104 us
    unnamed x7, local copies, waits for them, and re-layouts  6.86 us
    another operation x1, local copies, waits for them, and re-layouts, line_body(): outs = phase(2, jnp.stack(wide), *arrays)  5.63 us

profile of v1, /device:TPU:0, one launch (start us, length us, event | category | flops | bytes accessed | tf_op | source)
XLA Modules:
  0.0 121.8 jit_solution(3632061244274662269)
XLA Ops:
  0.7 0.9 select_reduce_fusion
  1.6 0.6 fusion.1
  2.2 0.8 compare_convert_fusion
  3.0 0.6 dynamic-slice_reduce_fusion
  4.3 0.7 fusion
  5.0 5.6 %stack.7.coef = f32[9]{0:T(128)} concatenate(f32[1]{0:T(128)} %bitcast, f32[1]{0:T(128)} %bitcast.1, f32[1]{0:T(128)} %bitcast.2, f32[1]{0:T(128)} %bitcast.3, f32[1]{0:T(128)} %bitcast.4, f32[1]{0:T(128)} %bitcast.5, f32[1]{0:T(128)} %bitcast.6, f32[1]{0:T(128)} %get-tuple-element.16, f32[1]{0:T(128)} %get-tuple-element.15), dimensions={0} | concatenate | bytes 72 | tf_op jit(solution)/shard_map/stack | solution.py:370
  10.6 104.3 %phase2.1 = (bf16[2048,512]{1,0:T(8,128)(2,1)}, bf16[2048,512]{1,0:T(8,128)(2,1)}, bf16[2048,512]{1,0:T(8,128)(2,1)}) custom-call(f32[9]{0:T(128)} %stack.7.coef, bf16[128,2048]{1,0:T(8,128)(2,1)} %bitcast.21, bf16[512,512]{1,0:T(8,128)(2,1)} %bitcast.22, bf16[2048,512]{1,0:T(8,128)(2,1)} %bitcast.18, bf16[2048,512]{1,0:T(8,128)(2,1)} %bitcast.19, ...), custom_call_target="tpu_custom_call" | custom-call | flops 6442450944 | bytes 14680064 | tf_op jit(solution)/shard_map/phase2/pallas_call | solution.py:332
  115.0 0.0 copy-start.1
  115.0 3.2 %copy.12 = bf16[1,2048,512]{2,1,0:T(8,128)(2,1)} copy(bf16[1,2048,512]{2,1,0:T(8,128)(2,1)} %bitcast.17) | data formatting | bytes 4194304
  118.2 0.0 copy-done.1
  118.2 0.0 copy-start
  118.2 1.3 %copy.13 = bf16[1,2048,512]{2,1,0:T(8,128)(2,1)} copy(bf16[1,2048,512]{2,1,0:T(8,128)(2,1)S(1)} %bitcast.16) | data formatting | bytes 4194304
  119.5 1.0 copy-done
  120.5 1.3 %copy.14 = bf16[1,2048,512]{2,1,0:T(8,128)(2,1)} copy(bf16[1,2048,512]{2,1,0:T(8,128)(2,1)S(1)} %bitcast.15) | data formatting | bytes 4194304
  (1 shorter events, 0.0 us)
Async XLA Ops:
  115.0 3.2 %copy-start.1 = (bf16[2048,512]{1,0:T(8,128)(2,1)S(1)}, bf16[2048,512]{1,0:T(8,128)(2,1)}, u32[]{:S(2)}) copy-start(bf16[2048,512]{1,0:T(8,128)(2,1)} %get-tuple-element.7) | copy-start | bytes 6291460
  118.2 2.3 %copy-start = (bf16[2048,512]{1,0:T(8,128)(2,1)S(1)}, bf16[2048,512]{1,0:T(8,128)(2,1)}, u32[]{:S(2)}) copy-start(bf16[2048,512]{1,0:T(8,128)(2,1)} %get-tuple-element.8) | copy-start | bytes 6291460

commit v2 on v1

--- a/solution.py
+++ b/solution.py
@@ -21,10 +21,35 @@
 BF16 = jnp.bfloat16
 
 
-def kernel(slots, coef, a_hbm, c_hbm, w_hbm, d_hbm, m_hbm, ow_hbm, od_hbm, om_hbm,
-           a, c, w, d, m, e, y1, y2, z, proj, normed, sens, gram, grads, cur, ow, od, om,
-           sent, sums, load, agx_s, agx_r, agc_s, agc_r, agf_s, agf_r, ex_s, ex_r,
-           e_s, e_r, y1_s, y1_r, y2_s, y2_r, z_s, z_r, out_s):
+def same(path, i, j):
+    return jnp.where(path[i] == path[j], 1.0, 0.0)
+
+
+def crossing(path, i):
+    other = 2 - 2 * (i // 2)
+    return jnp.maximum(same(path, i, other), same(path, i, other + 1))
+
+
+def others(i):
+    low = i // 2
+    return 2 - low, 3 - 3 * low
+
+
+def first_share(path, i):
+    near, far = others(i)
+    inner = crossing(path, near)
+    return inner * same(path, i, near) + (1.0 - inner) * same(path, i, far)
+
+
+def second_share(path, i):
+    near, far = others(i)
+    return crossing(path, near) * (1.0 - same(path, near, far)) * same(path, i, far)
+
+
+def phase_kernel(path, a_hbm, c_hbm, w_hbm, d_hbm, cur_hbm, sum_hbm, flag,
+                 a, c, w, d, e, x, y, z, proj, normed, sens, gram, grads, cur, summed,
+                 sent, sums, mark, load, agx_s, agx_r, agc_s, agc_r, agf_s, agf_r, ex_s, ex_r,
+                 e_s, e_r, y_s, y_r, z_s, z_r, out_s, mark_s, mark_r):
     tokens, width = a.shape
     columns = w.shape[1]
     shard = tokens // 4
@@ -34,6 +59,7 @@
 
     o = lax.axis_index("outer")
     s = lax.axis_index("seq")
+    part = lax.axis_index("group")
     core = s % 2
     chip = s // 2
     peers = (chip * 2 + 1 - core, (1 - chip) * 2 + core, (1 - chip) * 2 + 1 - core)
@@ -50,23 +76,24 @@
     for peer in peers:
         pl.semaphore_signal(barrier, inc=1, device_id={"seq": peer}, device_id_type=MESH)
     pl.semaphore_signal(barrier, inc=1, device_id={"outer": near}, device_id_type=MESH)
+    pl.semaphore_signal(barrier, inc=1, device_id={"group": 1 - part}, device_id_type=MESH)
 
     @pl.when(inner)
     def _():
         pl.semaphore_signal(barrier, inc=1, device_id={"outer": mid}, device_id_type=MESH)
 
     local = [pltpu.make_async_copy(x, y, load.at[k]) for k, (x, y) in enumerate(
-        ((a_hbm, a.at[pl.ds(pl.multiple_of(s * shard, shard), shard)]), (w_hbm, w), (c_hbm, c), (d_hbm, d), (m_hbm, m)))]
+        ((a_hbm, a.at[pl.ds(pl.multiple_of(s * shard, shard), shard)]), (w_hbm, w), (c_hbm, c), (d_hbm, d)))]
     for copy in local:
         copy.start()
 
     @pl.when(inner)
     def _():
+        pl.semaphore_wait(barrier, 6)
+
+    @pl.when(end)
+    def _():
         pl.semaphore_wait(barrier, 5)
-
-    @pl.when(end)
-    def _():
-        pl.semaphore_wait(barrier, 4)
 
     parts = 4
     piece = shard // parts
@@ -92,12 +119,8 @@
     def send_e(k):
         return remote(d_hbm.at[span(k)], e.at[span(k)], e_s.at[k], e_r.at[k], outer=near)
 
-    def send_y1(k):
-        return remote(d_hbm.at[span(k)] if slots == 2 else y2.at[span(k)], y1.at[span(k)],
-                      y1_s.at[k], y1_r.at[k], outer=mid)
-
-    def send_y2(k):
-        return remote(e.at[span(k)], y2.at[span(k)], y2_s.at[k], y2_r.at[k], outer=mid)
+    def send_y(k):
+        return remote(x.at[span(k)], y.at[span(k)], y_s.at[k], y_r.at[k], outer=mid)
 
     def send_z(k):
         return remote(z.at[span(k)], e.at[span(k)], z_s.at[k], z_r.at[k], outer=near)
@@ -112,33 +135,42 @@
     def _():
         loop(0, PIECES, lambda k: send_e(k).start())
 
-    if slots == 2:
+    need = crossing(path, 0) * crossing(path, 1) * (1.0 - same(path, 0, 1))
+    mark[0] = jnp.full((8, 128), need, F32)
+    tell = remote(mark.at[0], mark.at[1], mark_s, mark_r, group=1 - part)
+    tell.start()
+
+    own_cross = crossing(path, o)
+    x_own = own_cross
+    x_end = own_cross * same(path, o, near) + (1.0 - own_cross) * crossing(path, near)
+    pair = same(path, o, near)
+    take = first_share(path, o)
+    near_take = first_share(path, near)
+
+    def collected(k):
+        return pltpu.make_async_copy(summed.at[span(k)], sum_hbm.at[span(k)], out_s.at[k])
+
+    def combine(k):
+        send_e(k).wait_recv()
+        x[span(k)] = (x_end * e[span(k)].astype(F32) + x_own * d[span(k)].astype(F32)).astype(BF16)
+        send_y(k).start()
+
+    def pass_on(k):
+        send_y(k).wait_recv()
+        mine = d[span(k)].astype(F32)
+        across = y[span(k)].astype(F32)
+        z[span(k)] = (pair * mine + near_take * across).astype(BF16)
+        send_z(k).start()
+        summed[span(k)] = mine + pair * e[span(k)].astype(F32) + take * across
+        collected(k).start()
+
+    lag = 2
+
+    def tick(lo, hi):
         @pl.when(inner)
         def _():
-            loop(0, PIECES, lambda k: send_y1(k).start())
-
-    def combine(k):
-        send_e(k).wait_recv()
-        y2[span(k)] = (coef[7] * e[span(k)].astype(F32) + coef[8] * d[span(k)].astype(F32)).astype(BF16)
-        send_y1(k).start()
-
-    def pass_on(k):
-        send_y1(k).wait_recv()
-        total = coef[4] * d[span(k)].astype(F32) + coef[5] * y1[span(k)].astype(F32)
-        if slots == 2:
-            send_y2(k).wait_recv()
-            total = total + coef[6] * y2[span(k)].astype(F32)
-        z[span(k)] = total.astype(BF16)
-        send_z(k).start()
-
-    lag = 2
-
-    def tick(lo, hi):
-        if slots == 1:
-            @pl.when(inner)
-            def _():
-                loop(lo, min(hi, PIECES), combine)
-                loop(max(lo - lag, 0), hi - lag, pass_on)
+            loop(lo, hi, combine)
+            loop(max(lo - lag, 0), max(hi - lag, 0), pass_on)
 
     for copy in local:
         copy.wait()
@@ -242,58 +274,22 @@
         acc = jnp.dot(turned, grads[0], preferred_element_type=F32)
         for step in range(1, STEPS):
             acc = acc + jnp.dot(turned, grads[step], preferred_element_type=F32)
-        od[r, :] = (acc * (factor / STEPS)).astype(BF16)
         cur[r, :] = w[r, :].astype(F32) - acc * (inner_rate * factor)
     loop(0, width // 256, weight_rows)
-    delta_out = pltpu.make_async_copy(od, od_hbm, out_s.at[2, 0])
-    delta_out.start()
-
-    def outs(k):
-        return (pltpu.make_async_copy(ow.at[span(k)], ow_hbm.at[span(k)], out_s.at[0, k]),
-                pltpu.make_async_copy(om.at[span(k)], om_hbm.at[span(k)], out_s.at[1, k]))
-
-    def finish(k, summed):
-        outer_grad = summed * coef[0]
-        moment = beta_outer * m[span(k)].astype(F32) + outer_grad
-        direction = outer_grad + beta_outer * moment
-        om[span(k)] = moment.astype(BF16)
-        ow[span(k)] = (cur[span(k)] - (outer_rate * inner_rate * STEPS) * direction).astype(BF16)
-        for copy in outs(k):
-            copy.start()
-
-    def finish_inner(k):
-        summed = d[span(k)].astype(F32) + coef[1] * e[span(k)].astype(F32) + coef[2] * y1[span(k)].astype(F32)
-        if slots == 2:
-            summed = summed + coef[3] * y2[span(k)].astype(F32)
-        finish(k, summed)
+    trained = pltpu.make_async_copy(cur, cur_hbm, out_s.at[PIECES])
+    trained.start()
 
     @pl.when(inner)
     def _():
-        if slots == 2:
-            def relay(k):
-                send_e(k).wait_recv()
-                send_y2(k).start()
-            loop(0, PIECES, relay)
-
-            def both(k):
-                pass_on(k)
-                finish_inner(k)
-            loop(0, PIECES, both)
-        else:
-            done = points[-1][1]
-
-            def both(k):
-                @pl.when(k < PIECES)
-                def _():
-                    combine(k)
-                pass_on(k - lag)
-            loop(done, PIECES + lag, both)
-            loop(0, PIECES, finish_inner)
+        def both(k):
+            @pl.when(k < PIECES)
+            def _():
+                combine(k)
+            pass_on(k - lag)
+        loop(points[-1][1], PIECES + lag, both)
 
         def settle(k):
-            send_y1(k).wait_send()
-            if slots == 2:
-                send_y2(k).wait_send()
+            send_y(k).wait_send()
             send_z(k).wait_send()
         loop(0, PIECES, settle)
 
@@ -301,10 +297,13 @@
     def _():
         def last(k):
             send_z(k).wait_recv()
-            finish(k, d[span(k)].astype(F32) + e[span(k)].astype(F32))
+            summed[span(k)] = d[span(k)].astype(F32) + e[span(k)].astype(F32)
+            collected(k).start()
         loop(0, PIECES, last)
         loop(0, PIECES, lambda k: send_e(k).wait_send())
 
+    tell.wait()
+    flag[...] = mark[0] + mark[1]
     to_core.wait_send()
     for k in range(parts):
         to_chip(k).wait_send()
@@ -313,62 +312,193 @@
         for k in range(3):
             exchange(n, k).wait_send()
 
+    loop(0, PIECES, lambda k: collected(k).wait())
+    trained.wait()
+
+
+def second_kernel(path, d_hbm, sum_hbm, out_hbm, e, y, add, load, e_s, e_r, y_s, y_r, z_s, z_r, out_s):
+    width = y.shape[0]
+    rows = width // PIECES
+    o = lax.axis_index("outer")
+    near = o + 1 - 2 * (o % 2)
+    mid = 3 - o
+    inner = jnp.logical_or(o == 1, o == 2)
+    end = jnp.logical_or(o == 0, o == 3)
+
+    barrier = pltpu.get_barrier_semaphore()
+    pl.semaphore_signal(barrier, inc=1, device_id={"outer": near}, device_id_type=MESH)
+
+    @pl.when(inner)
+    def _():
+        pl.semaphore_signal(barrier, inc=1, device_id={"outer": mid}, device_id_type=MESH)
+        pl.semaphore_wait(barrier, 2)
+
+    @pl.when(end)
+    def _():
+        pl.semaphore_wait(barrier, 1)
+
+    def span(k):
+        return pl.ds(pl.multiple_of(k * rows, rows), rows)
+
+    def link(src, dst, send, recv, k, to):
+        return pltpu.make_async_remote_copy(
+            src_ref=src.at[span(k)], dst_ref=dst.at[span(k)], send_sem=send.at[k], recv_sem=recv.at[k],
+            device_id={"outer": to}, device_id_type=MESH)
+
+    def send_e(k):
+        return link(d_hbm, e, e_s, e_r, k, near)
+
+    def send_y(k):
+        return link(e, y, y_s, y_r, k, mid)
+
+    def send_z(k):
+        return link(y, y, z_s, z_r, k, near)
+
+    def loop(lo, hi, body):
+        def step(k, carry):
+            body(k)
+            return carry
+        lax.fori_loop(lo, hi, step, 0)
+
+    @pl.when(end)
+    def _():
+        loop(0, PIECES, lambda k: send_e(k).start())
+
+    fetch = pltpu.make_async_copy(sum_hbm, add, load)
+    fetch.start()
+    fetch.wait()
+    share = second_share(path, o)
+
     def written(k):
-        for copy in outs(k):
-            copy.wait()
-    loop(0, PIECES, written)
-    delta_out.wait()
-
-
-def phase(slots, coef, activations, cotangent, weights, earlier_delta, momentum):
+        return pltpu.make_async_copy(add.at[span(k)], out_hbm.at[span(k)], out_s.at[k])
+
+    def take(k):
+        add[span(k)] += share * y[span(k)].astype(F32)
+        written(k).start()
+
+    @pl.when(inner)
+    def _():
+        lag = 2
+
+        def relay(k):
+            @pl.when(k < PIECES)
+            def _():
+                send_e(k).wait_recv()
+                send_y(k).start()
+
+            @pl.when(k >= lag)
+            def _():
+                send_y(k - lag).wait_recv()
+                send_z(k - lag).start()
+                take(k - lag)
+        loop(0, PIECES + lag, relay)
+
+        def settle(k):
+            send_y(k).wait_send()
+            send_z(k).wait_send()
+        loop(0, PIECES, settle)
+
+    @pl.when(end)
+    def _():
+        def last(k):
+            send_z(k).wait_recv()
+            take(k)
+        loop(0, PIECES, last)
+        loop(0, PIECES, lambda k: send_e(k).wait_send())
+
+    loop(0, PIECES, lambda k: written(k).wait())
+
+
+def finish_kernel(path, w, m, cur, summed, new_weights, outer_delta, new_momentum):
+    o = lax.axis_index("outer")
+    size = same(path, o, 0) + same(path, o, 1) + same(path, o, 2) + same(path, o, 3)
+    share = 1.0 / jnp.full((1, w.shape[1]), size, F32)
+    outer_grad = summed[...] * share
+    moment = beta_outer * m[...].astype(F32) + outer_grad
+    direction = outer_grad + beta_outer * moment
+    new_momentum[...] = moment.astype(BF16)
+    outer_delta[...] = ((w[...].astype(F32) - cur[...]) * (1.0 / (inner_rate * STEPS))).astype(BF16)
+    new_weights[...] = (cur[...] - (outer_rate * inner_rate * STEPS) * direction).astype(BF16)
+
+
+ANY = pl.BlockSpec(memory_space=pl.ANY)
+SMEM = pl.BlockSpec(memory_space=pltpu.SMEM)
+dma = pltpu.SemaphoreType.DMA
+
+
+def phase(path, activations, cotangent, weights, earlier_delta):
     width, columns = weights.shape
     tokens = cotangent.shape[0]
-    any_spec = pl.BlockSpec(memory_space=pl.ANY)
     full = pltpu.VMEM((width, columns), BF16)
+    wide = pltpu.VMEM((width, columns), F32)
     plane = pltpu.VMEM((tokens, columns), F32)
-    dma = pltpu.SemaphoreType.DMA
     line = dma((PIECES,))
+    out = jax.ShapeDtypeStruct((width, columns), F32)
+    return pl.pallas_call(
+        phase_kernel,
+        out_shape=(out, out, jax.ShapeDtypeStruct((8, 128), F32)),
+        in_specs=[SMEM] + [ANY] * 4,
+        out_specs=(ANY, ANY, pl.BlockSpec(memory_space=pltpu.VMEM)),
+        scratch_shapes=[
+            pltpu.VMEM((tokens, width), BF16), pltpu.VMEM((tokens, columns), BF16),
+            full, full, full, full, full, full,
+            plane, plane, plane, pltpu.VMEM((tokens, tokens), BF16),
+            pltpu.VMEM((STEPS, tokens, columns), BF16), wide, wide,
+            pltpu.VMEM((2 * STEPS, 8, 128), F32), pltpu.VMEM((2 * STEPS, 3, 8, 128), F32),
+            pltpu.VMEM((2, 8, 128), F32),
+            dma((4,)), dma((4,)), dma((4,)), dma, dma, dma((4,)), dma((4,)),
+            dma((2 * STEPS, 3)), dma((2 * STEPS, 3)),
+            line, line, line, line, line, line, dma((PIECES + 1,)), dma, dma,
+        ],
+        compiler_params=pltpu.CompilerParams(
+            collective_id=1, has_side_effects=True, vmem_limit_bytes=48 * 1024 * 1024),
+        cost_estimate=pl.CostEstimate(
+            flops=12 * tokens * width * columns, bytes_accessed=14 * width * columns, transcendentals=0),
+        name="phase",
+    )(path, activations, cotangent, weights, earlier_delta)
+
+
+def second(path, earlier_delta, summed):
+    width, columns = summed.shape
+    full = pltpu.VMEM((width, columns), BF16)
+    line = dma((PIECES,))
+    return pl.pallas_call(
+        second_kernel,
+        out_shape=jax.ShapeDtypeStruct((width, columns), F32),
+        in_specs=[SMEM, ANY, ANY],
+        out_specs=ANY,
+        scratch_shapes=[full, full, pltpu.VMEM((width, columns), F32), dma] + [line] * 7,
+        compiler_params=pltpu.CompilerParams(
+            collective_id=2, has_side_effects=True, vmem_limit_bytes=32 * 1024 * 1024),
+        name="second",
+    )(path, earlier_delta, summed)
+
+
+def finish(path, weights, momentum, cur, summed):
+    width, columns = weights.shape
+    rows = 256
+    block = pl.BlockSpec((rows, columns), lambda k: (k, 0))
     out = jax.ShapeDtypeStruct((width, columns), BF16)
     return pl.pallas_call(
-        functools.partial(kernel, slots),
+        finish_kernel,
+        grid=(width // rows,),
         out_shape=(out, out, out),
-        in_specs=[pl.BlockSpec(memory_space=pltpu.SMEM)] + [any_spec] * 5,
-        out_specs=(any_spec,) * 3,
-        scratch_shapes=[
-            pltpu.VMEM((tokens, width), BF16), pltpu.VMEM((tokens, columns), BF16),
-            full, full, full, full, full, full, full,
-            plane, plane, plane, pltpu.VMEM((tokens, tokens), BF16),
-            pltpu.VMEM((STEPS, tokens, columns), BF16),
-            pltpu.VMEM((width, columns), F32), full, full, full,
-            pltpu.VMEM((2 * STEPS, 8, 128), F32), pltpu.VMEM((2 * STEPS, 3, 8, 128), F32),
-            dma((5,)), dma((4,)), dma((4,)), dma, dma, dma((4,)), dma((4,)),
-            dma((2 * STEPS, 3)), dma((2 * STEPS, 3)),
-            line, line, line, line, line, line, line, line, dma((3, PIECES)),
-        ],
-        compiler_params=pltpu.CompilerParams(
-            collective_id=slots, has_side_effects=True, vmem_limit_bytes=56 * 1024 * 1024),
-        cost_estimate=pl.CostEstimate(
-            flops=12 * tokens * width * columns, bytes_accessed=14 * width * columns, transcendentals=0),
-        name="phase%d" % slots,
-    )(coef, activations, cotangent, weights, earlier_delta, momentum)
+        in_specs=[SMEM, block, block, block, block],
+        out_specs=(block, block, block),
+        compiler_params=pltpu.CompilerParams(vmem_limit_bytes=24 * 1024 * 1024),
+        name="finish",
+    )(path, weights, momentum, cur, summed)
 
 
 def line_body(activations, cotangent, weights, earlier_delta, momentum, module_path):
-    shared = (module_path[:, None] == module_path[None, :]).astype(F32)
-    own = lax.axis_index("outer")
-    near = own + 1 - 2 * (own % 2)
-    mid, far = 3 - own, 3 - near
-    side = jnp.arange(4) // 2
-    crosses = jnp.max(jnp.where(side[:, None] != side[None, :], shared, 0.0), axis=1)
-
-    def pair(i, j):
-        return shared[i, j]
-
-    wide = [1.0 / jnp.sum(shared[own]), pair(own, near), pair(own, mid), pair(own, far),
-            pair(near, own), pair(near, mid), pair(near, far), crosses[near], crosses[own]]
-    arrays = (activations[0], cotangent[0], weights[0], earlier_delta[0], momentum[0])
-    outs = phase(2, jnp.stack(wide), *arrays)
-    return tuple(x[None] for x in outs)
+    delta = earlier_delta[0]
+    cur, summed, flag = phase(module_path, activations[0], cotangent[0], weights[0], delta)
+    outs = lax.cond(
+        flag[0, 0] > 0,
+        lambda t: finish(module_path, weights[0], momentum[0], cur, second(module_path, delta, t)),
+        lambda t: finish(module_path, weights[0], momentum[0], cur, t),
+        summed)
+    return tuple(t[None] for t in outs)
 
 
 def body(activations, cotangent, weights, earlier_delta, momentum, module_path):
@@ -437,7 +567,7 @@
     )
     def run(*args):
         sizes = (mesh.shape["outer"], mesh.shape["seq"], args[0].shape[1], args[2].shape[1])
-        fits = sizes[:2] == (4, 4) and sizes[2] == 512 and sizes[3] % 512 == 0 and sizes[3] <= 2048
+        fits = mesh.shape["group"] == 2 and sizes[:2] == (4, 4) and sizes[2] == 512 and sizes[3] % 512 == 0 and sizes[3] <= 2048
         chosen = line_body if fits else body
         return jax.shard_map(
             chosen, mesh=mesh, in_specs=in_specs, out_specs=out_specs, check_vma=False)(*args)

time: 122 us -> 82.2 us (0.67)
  Pallas kernels: 104 us -> 78 us
  local copies, waits for them, and re-layouts: 13.8 us -> 2.6 us
  other arithmetic: 2.32 us -> 0 us
    pallas_call x1 -> x2, Pallas kernels: 104 us -> 78 us  [the longest x1 73.2 us: phase(): pl.pallas_call(phase_kernel, out_shape=(out, out, jax.ShapeDtypeStruct((8...]
    another operation x1 -> x0, local copies, waits for them, and re-layouts: 5.63 us -> none  [line_body(): outs = phase(2, jnp.stack(wide), *arrays)]
    unnamed x7 -> x10, local copies, waits for them, and re-layouts: 6.86 us -> 2.09 us
    dynamic_slice x2 -> x0, local copies, waits for them, and re-layouts: 1.31 us -> none  [the longest x1 0.69 us: pair(): return shared[i, j]]
where the time goes in v2:
time: 82.2 us; the launch traced here: 81.9 us
  Pallas kernels  78 us (95%)
  local copies, waits for them, and re-layouts  2.6 us (3%)
  between operations  1.33 us (2%)
    pallas_call x1, Pallas kernels, phase(): pl.pallas_call(phase_kernel, out_shape=(out, out, jax.ShapeDtypeStruct((8...  73.2 us
    pallas_call x1, Pallas kernels, finish(): pl.pallas_call(finish_kernel, grid=(width // rows,), out_shape=(out, out,...  4.76 us
    unnamed x10, local copies, waits for them, and re-layouts  2.09 us

profile of v2, /device:TPU:0, one launch (start us, length us, event | category | flops | bytes accessed | tf_op | source)
XLA Modules:
  0.0 81.9 jit_solution(4085722552192073698)
XLA Ops:
  0.6 0.0 copy-start
  0.6 1.0 %copy-done = bf16[1,128,2048]{2,1,0:T(8,128)(2,1)S(1)} copy-done((bf16[1,128,2048]{2,1,0:T(8,128)(2,1)S(1)}, bf16[1,128,2048]{2,1,0:T(8,128)(2,1)}, u32[]{:S(2)}) %copy-start) | copy-done | bytes 524312
  1.7 0.0 copy-start.1
  1.7 1.0 %copy-done.1 = bf16[1,512,512]{2,1,0:T(8,128)(2,1)S(1)} copy-done((bf16[1,512,512]{2,1,0:T(8,128)(2,1)S(1)}, bf16[1,512,512]{2,1,0:T(8,128)(2,1)}, u32[]{:S(2)}) %copy-start.1) | copy-done | bytes 524312
  2.7 0.0 copy-start.2
  2.7 0.0 copy-start.3
  2.7 0.0 copy-start.4
  2.7 73.2 %phase.1 = (f32[2048,512]{1,0:T(8,128)S(1)}, f32[2048,512]{1,0:T(8,128)S(1)}, f32[8,128]{1,0:T(8,128)S(1)}) custom-call(s32[4]{0:T(128)} %path.1, bf16[128,2048]{1,0:T(8,128)(2,1)S(1)} %bitcast.12, bf16[512,512]{1,0:T(8,128)(2,1)S(1)} %bitcast.13, bf16[2048,512]{1,0:T(8,128)(2,1)} %bitcast.14, bf16[2048,512]{1,0:T(8,128)(2,1)} %bitcast.19), custom_call_target="tpu_custom_call" | custom-call | flops 6442450944 | bytes 14680064 | tf_op jit(solution)/shard_map/phase/pallas_call | solution.py:437
  76.0 0.5 slice.3
  77.1 0.0 copy-done.2
  77.2 0.0 copy-done.3
  77.2 0.0 copy-done.4
  77.2 4.8 %conditional.1 = ((bf16[2048,512]{1,0:T(8,128)(2,1)}, bf16[2048,512]{1,0:T(8,128)(2,1)}, bf16[2048,512]{1,0:T(8,128)(2,1)})) conditional(s32[]{:T(128)} %bitcast.4, (bf16[1,2048,512]{2,1,0:T(8,128)(2,1)S(1)}, bf16[1,2048,512]{2,1,0:T(8,128)(2,1)S(1)}, s32[4]{0:T(128)S(1)}, f32[2048,512]{1,0:T(8,128)S(1)}, ...), branch_computations={%region_0.0_spmd.clone, %region_1.0_spmd.clone} | conditional | bytes 8 | solution.py:496
  77.2 4.8 %finish.2 = (bf16[2048,512]{1,0:T(8,128)(2,1)}, bf16[2048,512]{1,0:T(8,128)(2,1)}, bf16[2048,512]{1,0:T(8,128)(2,1)}) custom-call(s32[4]{0:T(128)S(1)} %get-tuple-element.62.path, bf16[2048,512]{1,0:T(8,128)(2,1)S(1)} %bitcast.15, bf16[2048,512]{1,0:T(8,128)(2,1)S(1)} %bitcast.17, f32[2048,512]{1,0:T(8,128)S(1)} %get-tuple-element.65.cur, ...), custom_call_target="tpu_custom_call" | custom-call | tf_op jit(solution)/shard_map/cond/branch_0_fun/finish/pallas_call | solution.py:482
Async XLA Ops:
  0.6 1.0 %copy-start = (bf16[1,128,2048]{2,1,0:T(8,128)(2,1)S(1)}, bf16[1,128,2048]{2,1,0:T(8,128)(2,1)}, u32[]{:S(2)}) copy-start(bf16[1,128,2048]{2,1,0:T(8,128)(2,1)} %param.8) | copy-start | bytes 1572868
  1.7 1.0 %copy-start.1 = (bf16[1,512,512]{2,1,0:T(8,128)(2,1)S(1)}, bf16[1,512,512]{2,1,0:T(8,128)(2,1)}, u32[]{:S(2)}) copy-start(bf16[1,512,512]{2,1,0:T(8,128)(2,1)} %param.9) | copy-start | bytes 1572868
  2.7 74.4 %copy-start.2 = (bf16[1,2048,512]{2,1,0:T(8,128)(2,1)S(1)}, bf16[1,2048,512]{2,1,0:T(8,128)(2,1)}, u32[]{:S(2)}) copy-start(bf16[1,2048,512]{2,1,0:T(8,128)(2,1)} %param.10) | copy-start | bytes 6291460
  2.7 74.4 %copy-start.3 = (bf16[1,2048,512]{2,1,0:T(8,128)(2,1)S(1)}, bf16[1,2048,512]{2,1,0:T(8,128)(2,1)}, u32[]{:S(2)}) copy-start(bf16[1,2048,512]{2,1,0:T(8,128)(2,1)} %param.12) | copy-start | bytes 6291460
  2.7 74.4 %copy-start.4 = (s32[4]{0:T(128)S(1)}, s32[4]{0:T(128)}, u32[]{:S(2)}) copy-start(s32[4]{0:T(128)} %path.1) | copy-start | bytes 52

commit v3 on v2

--- a/solution.py
+++ b/solution.py
@@ -16,7 +16,7 @@
 beta_outer = 0.9
 
 MESH = pl.DeviceIdType.MESH
-PIECES = 16
+PIECES = 32
 F32 = jnp.float32
 BF16 = jnp.bfloat16
 
@@ -164,7 +164,7 @@
         summed[span(k)] = mine + pair * e[span(k)].astype(F32) + take * across
         collected(k).start()
 
-    lag = 2
+    lag = 4
 
     def tick(lo, hi):
         @pl.when(inner)
@@ -186,11 +186,11 @@
 
     to_core.wait_recv()
     project(chip)
-    tick(0, 1)
+    tick(0, 2)
     for k in range(parts):
         to_chip(k).wait_recv()
         forward(k).start()
-    tick(1, 3)
+    tick(2, 6)
     for k in range(parts):
         forward(k).wait_recv()
     project(1 - chip)
@@ -228,7 +228,7 @@
         gram[:, r] = (lax.dot_general(a[...], a[r, :], (((1,), (1,)), ((), ())), preferred_element_type=F32)
                       * (inner_rate / width)).astype(BF16)
 
-    points = ((3, 5), (5, 7), (7, 8), (8, 10), (10, 11), (11, 12))
+    points = ((6, 10), (10, 14), (14, 18), (18, 21), (21, 25), (25, 28))
     for step in range(STEPS):
         first, second = 2 * step, 2 * step + 1
 
@@ -275,6 +275,11 @@
         for step in range(1, STEPS):
             acc = acc + jnp.dot(turned, grads[step], preferred_element_type=F32)
         cur[r, :] = w[r, :].astype(F32) - acc * (inner_rate * factor)
+
+        @pl.when(jnp.logical_and(inner, k % 2 == 1))
+        def _():
+            combine(points[-1][1] + k // 2)
+            pass_on(points[-1][1] + k // 2 - lag)
     loop(0, width // 256, weight_rows)
     trained = pltpu.make_async_copy(cur, cur_hbm, out_s.at[PIECES])
     trained.start()
@@ -286,7 +291,7 @@
             def _():
                 combine(k)
             pass_on(k - lag)
-        loop(points[-1][1], PIECES + lag, both)
+        loop(points[-1][1] + width // 512, PIECES + lag, both)
 
         def settle(k):
             send_y(k).wait_send()
@@ -409,19 +414,39 @@
     loop(0, PIECES, lambda k: written(k).wait())
 
 
-def finish_kernel(path, w, m, cur, summed, new_weights, outer_delta, new_momentum):
+def finish_kernel(path, w, m, cur, summed, nw_hbm, od_hbm, nm_hbm, nw, od, nm, sems):
     o = lax.axis_index("outer")
     size = same(path, o, 0) + same(path, o, 1) + same(path, o, 2) + same(path, o, 3)
     share = 1.0 / jnp.full((1, w.shape[1]), size, F32)
-    outer_grad = summed[...] * share
-    moment = beta_outer * m[...].astype(F32) + outer_grad
-    direction = outer_grad + beta_outer * moment
-    new_momentum[...] = moment.astype(BF16)
-    outer_delta[...] = ((w[...].astype(F32) - cur[...]) * (1.0 / (inner_rate * STEPS))).astype(BF16)
-    new_weights[...] = (cur[...] - (outer_rate * inner_rate * STEPS) * direction).astype(BF16)
+    rows = w.shape[0] // 16
+
+    def outs(k):
+        r = pl.ds(pl.multiple_of(k * rows, rows), rows)
+        return [pltpu.make_async_copy(x.at[r], y.at[r], sems.at[n, k])
+                for n, (x, y) in enumerate(((nw, nw_hbm), (od, od_hbm), (nm, nm_hbm)))]
+
+    def step(k, carry):
+        r = pl.ds(pl.multiple_of(k * rows, rows), rows)
+        outer_grad = summed[r] * share
+        moment = beta_outer * m[r].astype(F32) + outer_grad
+        direction = outer_grad + beta_outer * moment
+        nm[r] = moment.astype(BF16)
+        od[r] = ((w[r].astype(F32) - cur[r]) * (1.0 / (inner_rate * STEPS))).astype(BF16)
+        nw[r] = (cur[r] - (outer_rate * inner_rate * STEPS) * direction).astype(BF16)
+        for copy in outs(k):
+            copy.start()
+        return carry
+    lax.fori_loop(0, 16, step, 0)
+
+    def settle(k, carry):
+        for copy in outs(k):
+            copy.wait()
+        return carry
+    lax.fori_loop(0, 16, settle, 0)
 
 
 ANY = pl.BlockSpec(memory_space=pl.ANY)
+HBM = pl.BlockSpec(memory_space=pltpu.HBM)
 SMEM = pl.BlockSpec(memory_space=pltpu.SMEM)
 dma = pltpu.SemaphoreType.DMA
 
@@ -437,7 +462,7 @@
     return pl.pallas_call(
         phase_kernel,
         out_shape=(out, out, jax.ShapeDtypeStruct((8, 128), F32)),
-        in_specs=[SMEM] + [ANY] * 4,
+        in_specs=[SMEM] + [HBM] * 4,
         out_specs=(ANY, ANY, pl.BlockSpec(memory_space=pltpu.VMEM)),
         scratch_shapes=[
             pltpu.VMEM((tokens, width), BF16), pltpu.VMEM((tokens, columns), BF16),
@@ -476,16 +501,14 @@
 
 def finish(path, weights, momentum, cur, summed):
     width, columns = weights.shape
-    rows = 256
-    block = pl.BlockSpec((rows, columns), lambda k: (k, 0))
     out = jax.ShapeDtypeStruct((width, columns), BF16)
     return pl.pallas_call(
         finish_kernel,
-        grid=(width // rows,),
         out_shape=(out, out, out),
-        in_specs=[SMEM, block, block, block, block],
-        out_specs=(block, block, block),
-        compiler_params=pltpu.CompilerParams(vmem_limit_bytes=24 * 1024 * 1024),
+        in_specs=[SMEM] + [pl.BlockSpec(memory_space=pltpu.VMEM)] * 4,
+        out_specs=(HBM,) * 3,
+        scratch_shapes=[pltpu.VMEM((width, columns), BF16)] * 3 + [dma((3, 16))],
+        compiler_params=pltpu.CompilerParams(vmem_limit_bytes=32 * 1024 * 1024),
         name="finish",
     )(path, weights, momentum, cur, summed)
 

time: 82.2 us -> 77.3 us (0.940)
  Pallas kernels: 78 us -> 73.1 us
    pallas_call x1, Pallas kernels: 73.2 us -> 69.4 us  [phase(): pl.pallas_call(phase_kernel, out_shape=(out, out, jax.ShapeDtypeStruct((8...]
    pallas_call x1, Pallas kernels: 4.76 us -> 3.68 us  [finish(): pl.pallas_call(finish_kernel, out_shape=(out, out, out), in_specs=[SMEM]...]
where the time goes in v3:
time: 77.3 us; the launch traced here: 77.1 us
  Pallas kernels  73.1 us (95%)
  local copies, waits for them, and re-layouts  2.6 us (3%)
  between operations  1.33 us (2%)
    pallas_call x1, Pallas kernels, phase(): pl.pallas_call(phase_kernel, out_shape=(out, out, jax.ShapeDtypeStruct((8...  69.4 us
    pallas_call x1, Pallas kernels, finish(): pl.pallas_call(finish_kernel, out_shape=(out, out, out), in_specs=[SMEM]...  3.68 us
    unnamed x10, local copies, waits for them, and re-layouts  2.09 us

profile of v3, /device:TPU:0, one launch (start us, length us, event | category | flops | bytes accessed | tf_op | source)
XLA Modules:
  0.0 77.1 jit_solution(11282302335418177437)
XLA Ops:
  0.6 0.0 copy-start
  0.6 1.0 %copy-done = bf16[1,128,2048]{2,1,0:T(8,128)(2,1)S(1)} copy-done((bf16[1,128,2048]{2,1,0:T(8,128)(2,1)S(1)}, bf16[1,128,2048]{2,1,0:T(8,128)(2,1)}, u32[]{:S(2)}) %copy-start) | copy-done | bytes 524312
  1.7 0.0 copy-start.1
  1.7 1.0 %copy-done.1 = bf16[1,512,512]{2,1,0:T(8,128)(2,1)S(1)} copy-done((bf16[1,512,512]{2,1,0:T(8,128)(2,1)S(1)}, bf16[1,512,512]{2,1,0:T(8,128)(2,1)}, u32[]{:S(2)}) %copy-start.1) | copy-done | bytes 524312
  2.7 0.0 copy-start.2
  2.7 0.0 copy-start.3
  2.7 0.0 copy-start.4
  2.7 69.4 %phase.1 = (f32[2048,512]{1,0:T(8,128)S(1)}, f32[2048,512]{1,0:T(8,128)S(1)}, f32[8,128]{1,0:T(8,128)S(1)}) custom-call(s32[4]{0:T(128)} %path.1, bf16[128,2048]{1,0:T(8,128)(2,1)S(1)} %bitcast.12, bf16[512,512]{1,0:T(8,128)(2,1)S(1)} %bitcast.13, bf16[2048,512]{1,0:T(8,128)(2,1)} %bitcast.14, bf16[2048,512]{1,0:T(8,128)(2,1)} %bitcast.19), custom_call_target="tpu_custom_call" | custom-call | flops 6442450944 | bytes 14680064 | tf_op jit(solution)/shard_map/phase/pallas_call | solution.py:462
  72.2 0.5 slice.3
  73.3 0.0 copy-done.2
  73.3 0.0 copy-done.3
  73.3 0.0 copy-done.4
  73.4 3.7 %conditional.1 = ((bf16[2048,512]{1,0:T(8,128)(2,1)}, bf16[2048,512]{1,0:T(8,128)(2,1)}, bf16[2048,512]{1,0:T(8,128)(2,1)})) conditional(s32[]{:T(128)} %bitcast.4, (bf16[1,2048,512]{2,1,0:T(8,128)(2,1)S(1)}, bf16[1,2048,512]{2,1,0:T(8,128)(2,1)S(1)}, s32[4]{0:T(128)S(1)}, f32[2048,512]{1,0:T(8,128)S(1)}, ...), branch_computations={%region_0.0_spmd.clone, %region_1.0_spmd.clone} | conditional | bytes 8 | solution.py:519
  73.4 3.7 %finish.2 = (bf16[2048,512]{1,0:T(8,128)(2,1)}, bf16[2048,512]{1,0:T(8,128)(2,1)}, bf16[2048,512]{1,0:T(8,128)(2,1)}) custom-call(s32[4]{0:T(128)S(1)} %get-tuple-element.62.path, bf16[2048,512]{1,0:T(8,128)(2,1)S(1)} %bitcast.15, bf16[2048,512]{1,0:T(8,128)(2,1)S(1)} %bitcast.17, f32[2048,512]{1,0:T(8,128)S(1)} %get-tuple-element.65.cur, ...), custom_call_target="tpu_custom_call" | custom-call | tf_op jit(solution)/shard_map/cond/branch_0_fun/finish/pallas_call | solution.py:505
Async XLA Ops:
  0.6 1.0 %copy-start = (bf16[1,128,2048]{2,1,0:T(8,128)(2,1)S(1)}, bf16[1,128,2048]{2,1,0:T(8,128)(2,1)}, u32[]{:S(2)}) copy-start(bf16[1,128,2048]{2,1,0:T(8,128)(2,1)} %param.8) | copy-start | bytes 1572868
  1.7 1.0 %copy-start.1 = (bf16[1,512,512]{2,1,0:T(8,128)(2,1)S(1)}, bf16[1,512,512]{2,1,0:T(8,128)(2,1)}, u32[]{:S(2)}) copy-start(bf16[1,512,512]{2,1,0:T(8,128)(2,1)} %param.9) | copy-start | bytes 1572868
  2.7 70.6 %copy-start.2 = (bf16[1,2048,512]{2,1,0:T(8,128)(2,1)S(1)}, bf16[1,2048,512]{2,1,0:T(8,128)(2,1)}, u32[]{:S(2)}) copy-start(bf16[1,2048,512]{2,1,0:T(8,128)(2,1)} %param.10) | copy-start | bytes 6291460
  2.7 70.6 %copy-start.3 = (bf16[1,2048,512]{2,1,0:T(8,128)(2,1)S(1)}, bf16[1,2048,512]{2,1,0:T(8,128)(2,1)}, u32[]{:S(2)}) copy-start(bf16[1,2048,512]{2,1,0:T(8,128)(2,1)} %param.12) | copy-start | bytes 6291460
  2.7 70.6 %copy-start.4 = (s32[4]{0:T(128)S(1)}, s32[4]{0:T(128)}, u32[]{:S(2)}) copy-start(s32[4]{0:T(128)} %path.1) | copy-start | bytes 52

commit v4 on v3

--- a/solution.py
+++ b/solution.py
@@ -16,9 +16,41 @@
 beta_outer = 0.9
 
 MESH = pl.DeviceIdType.MESH
-PIECES = 32
+FIRST = (2, 2, 4)
+EVEN = 13
+LAST = (4, 4, 2, 2, 2, 2)
+HEAD = len(FIRST)
+TAIL = HEAD + EVEN
+PIECES = TAIL + len(LAST)
 F32 = jnp.float32
 BF16 = jnp.bfloat16
+
+
+def loop(lo, hi, body):
+    def step(k, carry):
+        body(k)
+        return carry
+    for k in range(lo, min(hi, HEAD)):
+        body(k)
+    if max(lo, HEAD) < min(hi, TAIL):
+        lax.fori_loop(max(lo, HEAD), min(hi, TAIL), step, 0)
+    for k in range(max(lo, TAIL), hi):
+        body(k)
+
+
+def repeat(count, body):
+    def step(k, carry):
+        body(k)
+        return carry
+    lax.fori_loop(0, count, step, 0)
+
+
+def span_of(width, k):
+    rows = width // (EVEN + (sum(FIRST) + sum(LAST)) // 8)
+    sizes = FIRST + (8,) * EVEN + LAST
+    if isinstance(k, int):
+        return pl.ds(sum(sizes[:k]) * rows // 8, sizes[k] * rows // 8)
+    return pl.ds(pl.multiple_of((k - HEAD) * rows + sum(FIRST) * rows // 8, rows), rows)
 
 
 def same(path, i, j):
@@ -54,7 +86,6 @@
     columns = w.shape[1]
     shard = tokens // 4
     half = tokens // 2
-    rows = width // PIECES
     factor = 1.0 / width ** 0.5
 
     o = lax.axis_index("outer")
@@ -114,7 +145,7 @@
     to_core.start()
 
     def span(k):
-        return pl.ds(pl.multiple_of(k * rows, rows), rows)
+        return span_of(width, k)
 
     def send_e(k):
         return remote(d_hbm.at[span(k)], e.at[span(k)], e_s.at[k], e_r.at[k], outer=near)
@@ -124,12 +155,6 @@
 
     def send_z(k):
         return remote(z.at[span(k)], e.at[span(k)], z_s.at[k], z_r.at[k], outer=near)
-
-    def loop(lo, hi, body):
-        def step(k, carry):
-            body(k)
-            return carry
-        lax.fori_loop(lo, hi, step, 0)
 
     @pl.when(end)
     def _():
@@ -164,12 +189,17 @@
         summed[span(k)] = mine + pair * e[span(k)].astype(F32) + take * across
         collected(k).start()
 
-    lag = 4
-
-    def tick(lo, hi):
+    lag = 2
+
+    place = [0]
+
+    def tick(count):
+        lo, hi = place[0], place[0] + count
+        place[0] = hi
+
         @pl.when(inner)
         def _():
-            loop(lo, hi, combine)
+            loop(lo, min(hi, PIECES), combine)
             loop(max(lo - lag, 0), max(hi - lag, 0), pass_on)
 
     for copy in local:
@@ -182,18 +212,22 @@
         def one(k):
             cols = pl.ds(pl.multiple_of(k * tile, tile), tile)
             proj[r, cols] = jnp.dot(a[r, :], w[:, cols], preferred_element_type=F32) * factor
-        loop(0, columns // tile, one)
+        repeat(columns // tile, one)
 
     to_core.wait_recv()
+    tick(2)
     project(chip)
-    tick(0, 2)
+    tick(2)
     for k in range(parts):
         to_chip(k).wait_recv()
         forward(k).start()
-    tick(2, 6)
+        if k % 2 == 0:
+            tick(1)
+    tick(1)
     for k in range(parts):
         forward(k).wait_recv()
     project(1 - chip)
+    tick(1)
 
     group = 128
     groups = tokens // group
@@ -228,18 +262,17 @@
         gram[:, r] = (lax.dot_general(a[...], a[r, :], (((1,), (1,)), ((), ())), preferred_element_type=F32)
                       * (inner_rate / width)).astype(BF16)
 
-    points = ((6, 10), (10, 14), (14, 18), (18, 21), (21, 25), (25, 28))
     for step in range(STEPS):
         first, second = 2 * step, 2 * step + 1
 
         def squares(g):
             p = proj[rows_at(g), :]
             sent[first, pl.ds(g, 1), :] = to_row(jnp.sum(p * p, axis=1, keepdims=True))
-        loop(0, groups, squares)
+        repeat(groups, squares)
         post(first)
         if step == 0:
-            loop(0, tokens // 256, gram_tile)
-        tick(*points[first])
+            repeat(tokens // 256, gram_tile)
+        tick(1)
         collect(first)
 
         def inverse(g):
@@ -252,21 +285,22 @@
             normed[rows_at(g), :] = n
             sens[rows_at(g), :] = out
             sent[second, pl.ds(g, 1), :] = to_row(jnp.sum(out * n, axis=1, keepdims=True))
-        loop(0, groups, sensitivity)
+        repeat(groups, sensitivity)
         post(second)
-        tick(*points[second])
+        tick(1)
         collect(second)
 
         def gradient(g):
             mixed = to_column(total(second, g) / width)
             grads[step, rows_at(g), :] = (
                 (sens[rows_at(g), :] - normed[rows_at(g), :] * mixed) * inverse(g)).astype(BF16)
-        loop(0, groups, gradient)
+        repeat(groups, gradient)
         if step < STEPS - 1:
             def descend(k):
                 cols = pl.ds(pl.multiple_of(k * 256, 256), 256)
                 proj[:, cols] -= jnp.dot(gram[...], grads[step, :, cols], preferred_element_type=F32)
-            loop(0, columns // 256, descend)
+            repeat(columns // 256, descend)
+        tick(1)
 
     def weight_rows(k):
         r = pl.ds(pl.multiple_of(k * 256, 256), 256)
@@ -276,22 +310,18 @@
             acc = acc + jnp.dot(turned, grads[step], preferred_element_type=F32)
         cur[r, :] = w[r, :].astype(F32) - acc * (inner_rate * factor)
 
-        @pl.when(jnp.logical_and(inner, k % 2 == 1))
-        def _():
-            combine(points[-1][1] + k // 2)
-            pass_on(points[-1][1] + k // 2 - lag)
-    loop(0, width // 256, weight_rows)
+    for quarter in range(4):
+        repeat(width // 1024, lambda k: weight_rows(quarter * (width // 1024) + k))
+        tick(1)
     trained = pltpu.make_async_copy(cur, cur_hbm, out_s.at[PIECES])
     trained.start()
 
     @pl.when(inner)
     def _():
-        def both(k):
-            @pl.when(k < PIECES)
-            def _():
+        for k in range(place[0], PIECES + lag):
+            if k < PIECES:
                 combine(k)
             pass_on(k - lag)
-        loop(points[-1][1] + width // 512, PIECES + lag, both)
 
         def settle(k):
             send_y(k).wait_send()
@@ -323,7 +353,6 @@
 
 def second_kernel(path, d_hbm, sum_hbm, out_hbm, e, y, add, load, e_s, e_r, y_s, y_r, z_s, z_r, out_s):
     width = y.shape[0]
-    rows = width // PIECES
     o = lax.axis_index("outer")
     near = o + 1 - 2 * (o % 2)
     mid = 3 - o
@@ -343,7 +372,7 @@
         pl.semaphore_wait(barrier, 1)
 
     def span(k):
-        return pl.ds(pl.multiple_of(k * rows, rows), rows)
+        return span_of(width, k)
 
     def link(src, dst, send, recv, k, to):
         return pltpu.make_async_remote_copy(
@@ -359,12 +388,6 @@
     def send_z(k):
         return link(y, y, z_s, z_r, k, near)
 
-    def loop(lo, hi, body):
-        def step(k, carry):
-            body(k)
-            return carry
-        lax.fori_loop(lo, hi, step, 0)
-
     @pl.when(end)
     def _():
         loop(0, PIECES, lambda k: send_e(k).start())
@@ -386,17 +409,29 @@
         lag = 2
 
         def relay(k):
-            @pl.when(k < PIECES)
-            def _():
-                send_e(k).wait_recv()
-                send_y(k).start()
-
-            @pl.when(k >= lag)
-            def _():
-                send_y(k - lag).wait_recv()
-                send_z(k - lag).start()
-                take(k - lag)
-        loop(0, PIECES + lag, relay)
+            send_e(k).wait_recv()
+            send_y(k).start()
+
+        def take_on(k):
+            send_y(k).wait_recv()
+            send_z(k).start()
+            take(k)
+
+        def both(k):
+            relay(k)
+            take_on(k - lag)
+        for k in range(HEAD):
+            relay(k)
+            if k >= lag:
+                take_on(k - lag)
+        for k in range(HEAD, HEAD + lag):
+            relay(k)
+            take_on(k - lag)
+        loop(HEAD + lag, TAIL, both)
+        for k in range(TAIL, PIECES + lag):
+            if k < PIECES:
+                relay(k)
+            take_on(k - lag)
 
         def settle(k):
             send_y(k).wait_send()

time: 77.3 us -> 73.6 us (0.952)
  Pallas kernels: 73.1 us -> 69.4 us
    pallas_call x1, Pallas kernels: 69.4 us -> 65.8 us  [phase(): pl.pallas_call(phase_kernel, out_shape=(out, out, jax.ShapeDtypeStruct((8...]
where the time goes in v4:
time: 73.6 us; the launch traced here: 73.4 us
  Pallas kernels  69.4 us (94%)
  local copies, waits for them, and re-layouts  2.6 us (4%)
  between operations  1.33 us (2%)
    pallas_call x1, Pallas kernels, phase(): pl.pallas_call(phase_kernel, out_shape=(out, out, jax.ShapeDtypeStruct((8...  65.8 us
    pallas_call x1, Pallas kernels, finish(): pl.pallas_call(finish_kernel, out_shape=(out, out, out), in_specs=[SMEM]...  3.68 us
    unnamed x10, local copies, waits for them, and re-layouts  2.09 us

profile of v4, /device:TPU:0, one launch (start us, length us, event | category | flops | bytes accessed | tf_op | source)
XLA Modules:
  0.0 73.4 jit_solution(17906530131444553465)
XLA Ops:
  0.6 0.0 copy-start
  0.6 1.0 %copy-done = bf16[1,128,2048]{2,1,0:T(8,128)(2,1)S(1)} copy-done((bf16[1,128,2048]{2,1,0:T(8,128)(2,1)S(1)}, bf16[1,128,2048]{2,1,0:T(8,128)(2,1)}, u32[]{:S(2)}) %copy-start) | copy-done | bytes 524312
  1.7 0.0 copy-start.1
  1.7 1.0 %copy-done.1 = bf16[1,512,512]{2,1,0:T(8,128)(2,1)S(1)} copy-done((bf16[1,512,512]{2,1,0:T(8,128)(2,1)S(1)}, bf16[1,512,512]{2,1,0:T(8,128)(2,1)}, u32[]{:S(2)}) %copy-start.1) | copy-done | bytes 524312
  2.7 0.0 copy-start.2
  2.7 0.0 copy-start.3
  2.7 0.0 copy-start.4
  2.7 65.8 %phase.1 = (f32[2048,512]{1,0:T(8,128)S(1)}, f32[2048,512]{1,0:T(8,128)S(1)}, f32[8,128]{1,0:T(8,128)S(1)}) custom-call(s32[4]{0:T(128)} %path.1, bf16[128,2048]{1,0:T(8,128)(2,1)S(1)} %bitcast.12, bf16[512,512]{1,0:T(8,128)(2,1)S(1)} %bitcast.13, bf16[2048,512]{1,0:T(8,128)(2,1)} %bitcast.14, bf16[2048,512]{1,0:T(8,128)(2,1)} %bitcast.19), custom_call_target="tpu_custom_call" | custom-call | flops 6442450944 | bytes 14680064 | tf_op jit(solution)/shard_map/phase/pallas_call | solution.py:497
  68.5 0.5 slice.3
  69.7 0.0 copy-done.2
  69.7 0.0 copy-done.3
  69.7 0.0 copy-done.4
  69.7 3.7 %conditional.1 = ((bf16[2048,512]{1,0:T(8,128)(2,1)}, bf16[2048,512]{1,0:T(8,128)(2,1)}, bf16[2048,512]{1,0:T(8,128)(2,1)})) conditional(s32[]{:T(128)} %bitcast.4, (bf16[1,2048,512]{2,1,0:T(8,128)(2,1)S(1)}, bf16[1,2048,512]{2,1,0:T(8,128)(2,1)S(1)}, s32[4]{0:T(128)S(1)}, f32[2048,512]{1,0:T(8,128)S(1)}, ...), branch_computations={%region_0.0_spmd.clone, %region_1.0_spmd.clone} | conditional | bytes 8 | solution.py:554
  69.7 3.7 %finish.2 = (bf16[2048,512]{1,0:T(8,128)(2,1)}, bf16[2048,512]{1,0:T(8,128)(2,1)}, bf16[2048,512]{1,0:T(8,128)(2,1)}) custom-call(s32[4]{0:T(128)S(1)} %get-tuple-element.62.path, bf16[2048,512]{1,0:T(8,128)(2,1)S(1)} %bitcast.15, bf16[2048,512]{1,0:T(8,128)(2,1)S(1)} %bitcast.17, f32[2048,512]{1,0:T(8,128)S(1)} %get-tuple-element.65.cur, ...), custom_call_target="tpu_custom_call" | custom-call | tf_op jit(solution)/shard_map/cond/branch_0_fun/finish/pallas_call | solution.py:540
Async XLA Ops:
  0.6 1.0 %copy-start = (bf16[1,128,2048]{2,1,0:T(8,128)(2,1)S(1)}, bf16[1,128,2048]{2,1,0:T(8,128)(2,1)}, u32[]{:S(2)}) copy-start(bf16[1,128,2048]{2,1,0:T(8,128)(2,1)} %param.8) | copy-start | bytes 1572868
  1.7 1.0 %copy-start.1 = (bf16[1,512,512]{2,1,0:T(8,128)(2,1)S(1)}, bf16[1,512,512]{2,1,0:T(8,128)(2,1)}, u32[]{:S(2)}) copy-start(bf16[1,512,512]{2,1,0:T(8,128)(2,1)} %param.9) | copy-start | bytes 1572868
  2.7 66.9 %copy-start.2 = (bf16[1,2048,512]{2,1,0:T(8,128)(2,1)S(1)}, bf16[1,2048,512]{2,1,0:T(8,128)(2,1)}, u32[]{:S(2)}) copy-start(bf16[1,2048,512]{2,1,0:T(8,128)(2,1)} %param.10) | copy-start | bytes 6291460
  2.7 67.0 %copy-start.3 = (bf16[1,2048,512]{2,1,0:T(8,128)(2,1)S(1)}, bf16[1,2048,512]{2,1,0:T(8,128)(2,1)}, u32[]{:S(2)}) copy-start(bf16[1,2048,512]{2,1,0:T(8,128)(2,1)} %param.12) | copy-start | bytes 6291460
  2.7 67.0 %copy-start.4 = (s32[4]{0:T(128)S(1)}, s32[4]{0:T(128)}, u32[]{:S(2)}) copy-start(s32[4]{0:T(128)} %path.1) | copy-start | bytes 52
